TPU v7x, 512 devices: a whole 4x8x8 slice. The times are simulated.
512 devices in a mesh: row: 16 (over z_lo, x), col: 32 (over z_hi, y, core).
Axes of the slice: x: 4, y: 8, z: 8 (z_hi: 2, z_lo: 4; z = z_hi * 4 + z_lo), core: 2. Of those that a mesh axis runs over, the one named last changes fastest.
Arguments:
- front: float32 [4, 4096, 2, 8192], P(None, 'row', None, 'col'), may hold values from -6 to 6
- contrib: float32 [1, 4096, 1, 8192], P(None, 'row', None, 'col'), may hold values from -6 to 6
- child_map: int32 [2, 16], replicated, may hold values from 0 to 63, as said below
- pattern: int32 [2, 16, 16], replicated, may hold values 0 or 1
- inverse: float32 [1024, 1024], P('col'), as said below
Outputs:
- updated: float32 [4, 4096, 2, 8192], P(None, 'row', None, 'col')
Inputs may be any that keep to these rules, and one draw needn't show every extreme that they name: Each row of child_map (each child) holds 16 distinct parent blocks, and child_map[h, a] leaves the same remainder modulo 16 as a. `inverse`: lower triangular with a positive diagonal.
All inputs are finite; a program needn't handle non-finite values.
Results may differ from a plain program's by a relative error of at most 0.000098.
Values sent between devices are 32-bit elements; how exact they have to be, the bound alone decides.
A program may use at most 64 MiB of HBM per device.

v0:
```python
import jax
import jax.numpy as jnp
from jax import lax
from jax.sharding import PartitionSpec as P

PANEL = 1024


HIGHEST = lax.Precision.HIGHEST


def from_partner(shard, axis, bit):
    return lax.ppermute(shard, axis, [(i, i ^ 1 << bit) for i in range(lax.axis_size(axis))])


def broadcast(value, axis, source):
    kept = jnp.where(lax.axis_index(axis) == source, value, 0).astype(value.dtype)
    return lax.psum(kept, axis)


def place_child(
    blocks,
    child_index,
    row_index,
    col_index,
    child_map,
    pattern,
    row_count,
    col_count,
    row_slots,
    col_slots,
):
    half_count = col_count // 2
    slot_ids = jnp.arange(blocks.shape[0])
    row_child = slot_ids * row_count + row_index
    col_child = slot_ids * half_count + col_index % half_count
    parents = child_map[child_index]
    row_parent = parents[row_child]
    col_parent = parents[col_child]
    keep_mask = pattern[child_index][row_child[:, None], col_child[None, :]].astype(jnp.float32)
    row_pick = (row_parent[:, None] // row_count == jnp.arange(row_slots)[None, :]).astype(
        jnp.float32
    )
    col_owned = (col_parent[:, None] // col_count == jnp.arange(col_slots)[None, :]) & (
        col_parent[:, None] % col_count == col_index
    )
    col_pick = col_owned.astype(jnp.float32)
    masked = blocks * keep_mask[:, None, :, None]
    row_moved = jnp.einsum("ip,iujv->pujv", row_pick, masked, precision=HIGHEST)
    return jnp.einsum("pujv,jq->puqv", row_moved, col_pick, precision=HIGHEST)


def body(front, contrib, child_map, pattern, inverse):
    row_slots = front.shape[0]
    block_size = front.shape[1]
    col_slots = front.shape[2]
    row_count = lax.axis_size("row")
    col_count = lax.axis_size("col")
    half_count = col_count // 2
    row_index = lax.axis_index("row")
    col_index = lax.axis_index("col")
    own_child = col_index // half_count
    partner = from_partner(contrib, "col", half_count.bit_length() - 1)
    assembled = front + place_child(
        contrib,
        own_child,
        row_index,
        col_index,
        child_map,
        pattern,
        row_count,
        col_count,
        row_slots,
        col_slots,
    )
    assembled = assembled + place_child(
        partner,
        1 - own_child,
        row_index,
        col_index,
        child_map,
        pattern,
        row_count,
        col_count,
        row_slots,
        col_slots,
    )
    panel_blocks = PANEL // block_size
    pieces = []
    for column_block in range(panel_blocks):
        pieces.append(broadcast(assembled[:, :, 0, :], "col", column_block))
    panel_rows = jnp.concatenate(pieces, axis=2).reshape(row_slots * block_size, PANEL)
    factor_part = jnp.dot(panel_rows, inverse.T, precision=HIGHEST)
    factor_rows = lax.all_gather(factor_part, "col", axis=1, tiled=True)
    factor_blocks = factor_rows.reshape(row_slots, block_size, PANEL)
    grouped = factor_blocks.reshape(col_slots, col_count // row_count, block_size, PANEL)
    chosen = lax.dynamic_index_in_dim(grouped, col_index // row_count, 1, keepdims=False)
    transposed = broadcast(chosen, "row", col_index % row_count)
    update = jnp.einsum("iuk,jvk->iujv", factor_blocks, transposed, precision=HIGHEST)
    row_global = jnp.arange(row_slots) * row_count + row_index
    col_global = jnp.arange(col_slots) * col_count + col_index
    trailing = (row_global[:, None, None, None] >= panel_blocks) & (
        col_global[None, None, :, None] >= panel_blocks
    )
    in_panel = col_global[None, None, :, None] < panel_blocks
    start = jnp.minimum(col_index, panel_blocks - 1) * block_size
    panel_piece = lax.dynamic_slice_in_dim(factor_blocks, start, block_size, 2)
    return jnp.where(
        in_panel, panel_piece[:, :, None, :], jnp.where(trailing, assembled - update, assembled)
    )


def solution(mesh):
    return jax.shard_map(
        body,
        mesh=mesh,
        in_specs=(
            P(None, "row", None, "col"),
            P(None, "row", None, "col"),
            P(),
            P(),
            P("col", None),
        ),
        out_specs=P(None, "row", None, "col"),
        check_vma=False,
    )
```

profile of v0, /device:TPU:8, one launch (start us, length us, event | category | flops | bytes accessed | tf_op | source)
XLA Modules:
  0.0 725.1 jit_solution(1253907933498729551)
XLA Ops:
  6.5 0.0 copy-start
  6.5 0.0 all-reduce.6.cloned.1.call-start
  6.5 11.0 %collective-permute-start = (f32[1,256,1,256]{3,2,1,0:T(1,128)}, f32[1,256,1,256]{3,2,1,0:T(1,128)S(1)}, u32[]{:S(2)}, u32[]{:S(2)}) collective-permute-start(f32[1,256,1,256]{3,2,1,0:T(1,128)} %param.6), channel_id=1, source_target_pairs={{0,16},{1,17},{2,18},{3,19},{4,20},{5,21},{6,22},{7,23},{8,24},{9,... | collective-permute-start | bytes 786440 | tf_op jit(solution)/shard_map/ppermute | solution.py:13
  17.6 1.5 fusion.17
  21.7 0.1 add_bitcast_fusion
  21.8 0.6 fusion.18
  23.6 1.4 fusion.16
  25.6 1.0 broadcast_multiply_fusion.3
  34.7 0.0 copy-start.1
  34.8 0.0 collective-permute-done
  34.9 0.2 broadcast_multiply_fusion
  35.1 1.2 copy-done.1
  36.3 0.3 bitcast_add_fusion
  36.6 1.1 fusion.8
  37.7 1.7 fusion.9
  39.4 0.0 all-reduce.6.cloned.1.call-update
  39.5 0.0 all-gather.2.cloned.1.call-start
  39.5 351.0 %all-reduce.6.cloned.1.call-done = (f32[4,256,256]{2,1,0:T(8,128)}, f32[4,256,256]{2,1,0:T(8,128)}, f32[4,256,256]{2,1,0:T(8,128)}, f32[4,256,256]{2,1,0:T(8,128)}) async-done(((f32[4,256,256]{2,1,0:T(8,128)}, f32[4,256,256]{2,1,0:T(8,128)}, f32[4,256,256]{2,1,0:T(8,128)}, f32[4,256,256]{2,1,0:T(8,128)}), (f32[4,256,256]{2,1,0:T(8,128)}, f32[4,256,256]{2,1,0:T(8,128)}, f32[4,256,256]{2,1,0:T(8,128)}, ...) | async-done | bytes 4194320 | tf_op jit(solution)/shard_map/psum | solution.py:18
  390.5 2.8 pad_maximum_fusion
  393.3 0.0 copy-done
  393.3 4.6 fusion.19
  397.9 0.0 all-gather.2.cloned.1.call-update
  397.9 0.2 all-reduce.4.cloned.1.call-start
  398.1 112.1 %all-gather.2.cloned.1.call-done = f32[1024,1024]{0,1:T(8,128)} async-done(((f32[1024,32]{0,1:T(8,128)}), f32[1024,1024]{0,1:T(8,128)}) %all-gather.2.cloned.1.call-update) | async-done | bytes 4194320 | tf_op jit(solution)/shard_map/all_gather | solution.py:94
  510.2 6.6 reshape_reshape.3
  516.8 5.3 constant_dynamic-slice_fusion.1
  522.1 6.1 copy.20
  528.2 1.6 select_bitcast_fusion
  529.8 0.0 all-reduce.4.cloned.1.call-update
  529.8 0.1 broadcast_and_fusion
  529.9 5.7 reshape.186
  535.6 1.4 constant_dynamic-slice_fusion
  537.0 1.4 copy.11
  538.4 160.9 %all-reduce.4.cloned.1.call-done = f32[2,256,1024]{2,1,0:T(8,128)} async-done(((f32[2,256,1024]{2,1,0:T(8,128)}), f32[2,256,1024]{2,1,0:T(8,128)}) %all-reduce.4.cloned.1.call-update) | async-done | bytes 2097168 | tf_op jit(solution)/shard_map/psum | solution.py:18
  699.2 16.4 %fusion.2 = f32[4,256,2,256]{3,1,2,0:T(8,128)S(1)} fusion(f32[4,256,2,256]{3,1,2,0:T(8,128)S(1)} %bitcast_add_fusion, f32[2,256,1024]{2,1,0:T(8,128)} %all-reduce.4.cloned.1.call-done, f32[4,256,1024,1]{1,0,2,3:T(4,128)} %bitcast.80, f32[4,256,256]{2,1,0:T(8,128)} %copy.11, pred[2]{0:T(512)(128)(4,1)S(1)} %get-tuple-element.87, ...), kind=kOutput, calls=%fused_computation.4 | convolution fusion | flops 6444023808 | bytes 11534346 | tf_op jit(solution)/shard_map/iuk,jvk->iujv/dot_general | solution.py:99
  715.6 2.9 copy.14
  (8 shorter events, 0.1 us)
Async XLA Ops:
  6.5 386.7 %copy-start = (f32[32,1024]{1,0:T(8,128)S(1)}, f32[32,1024]{1,0:T(8,128)}, u32[]{:S(2)}) copy-start(f32[32,1024]{1,0:T(8,128)} %param.9) | copy-start | bytes 393220
  6.5 383.9 %all-reduce.6.cloned.1.call-start = ((), (), s32[]{:S(2)}) async-start(), calls=%async_computation.2 | async-start | bytes 8388608 | tf_op jit(solution)/shard_map/psum | solution.py:18
  6.5 28.2 %collective-permute-start = (f32[1,256,1,256]{3,2,1,0:T(1,128)}, f32[1,256,1,256]{3,2,1,0:T(1,128)S(1)}, u32[]{:S(2)}, u32[]{:S(2)}) collective-permute-start(f32[1,256,1,256]{3,2,1,0:T(1,128)} %param.6), channel_id=1, source_target_pairs={{0,16},{1,17},{2,18},{3,19},{4,20},{5,21},{6,22},{7,23},{8,24},{9,... | collective-permute-start | bytes 786440 | tf_op jit(solution)/shard_map/ppermute | solution.py:13
  34.7 1.6 copy-start.1
  39.5 470.7 %all-gather.2.cloned.1.call-start = ((), (), s32[]{:S(2)}) async-start(), calls=%async_computation | async-start | bytes 4325376 | tf_op jit(solution)/shard_map/all_gather | solution.py:94
  397.9 301.4 %all-reduce.4.cloned.1.call-start = ((), (), s32[]{:S(2)}) async-start(), calls=%async_computation.1 | async-start | bytes 4194304 | tf_op jit(solution)/shard_map/psum | solution.py:18
Sparse Core Ops, SparseCore 0:
  39.6 350.8 all-reduce.5
  398.0 112.1 all-gather.1
  529.9 169.2 all-reduce.3
where the time goes:
time: 726 us; the launch traced here: 725 us
  waiting for transfers between devices  624 us (86%)
  local copies, waits for them, and re-layouts  34 us (5%)
  between operations  25.9 us (4%)
  matrix products  21 us (3%)
  starting transfers between devices  11.3 us (2%)
  other arithmetic  8.95 us (1%)
    psum x2, waiting for transfers between devices, broadcast(): return lax.psum(kept, axis)  512 us
    all_gather x1, waiting for transfers between devices, body(): factor_rows = lax.all_gather(factor_part, 'col', axis=1, tiled=True)  112 us
    dot_general x1, matrix products, body(): jnp.einsum('iuk,jvk->iujv', factor_blocks, transposed, precision=HIGHEST)  16.4 us
  transfers between devices with their start and end apart: 4, of which 3 were waited for; matrix products, arithmetic and copies ran while one was open for 2% of the time, Pallas kernels for 0%

commit v1 on v0

v1 whole, which is shorter than its diff:
```python
import functools

import jax
import jax.numpy as jnp
from jax import lax
from jax.experimental import pallas as pl
from jax.experimental.pallas import tpu as pltpu
from jax.sharding import PartitionSpec as P

MESH = pl.DeviceIdType.MESH
F32 = jnp.float32
BF16 = jnp.bfloat16

BLK = 256
ROWS = 1024
CH = 64
NCH = ROWS // CH
PER_SLOT = BLK // CH
HOP_NUM, HOP_DEN = 5, 2
R_OFF = 3
GRP = 128
MAX_HOPS = 14
STEPS = NCH + (MAX_HOPS * HOP_NUM) // HOP_DEN + R_OFF + 1


def nt_dot(a, b):
    return lax.dot_general(a, b, (((1,), (1,)), ((), ())), preferred_element_type=F32)


def split(x):
    hi = x.astype(BF16)
    return hi, (x - hi.astype(F32)).astype(BF16)


def kernel(
    front, contrib, cmap, pattern, inv, out,
    fac, facc, pan, cpart, invx, wbuf, wh, wl, fh, fl, ch, cl,
    r_recv, c_recv, a_recv, w_recv, x_recv,
    fwd_s, rev_s, cross_s, sib_s, c_s, a_s, w_s, x_s,
):
    r = lax.axis_index("row")
    c = lax.axis_index("col")
    x, zlo = lax.rem(r, 4), r // 4
    zhi, y, core = c // 16, lax.rem(c // 2, 8), lax.rem(c, 2)
    n0 = lax.rem(c, 16) // 8

    def dev(x_, zlo_, zhi_, y_, core_):
        return (zlo_ * 4 + x_, zhi_ * 16 + y_ * 2 + core_)

    y_up = dev(x, zlo, zhi, lax.rem(y + 1, 8), core)
    y_dn = dev(x, zlo, zhi, lax.rem(y + 7, 8), core)
    sib = dev(x, zlo, zhi, y, 1 - core)
    part = dev(x, zlo, 1 - zhi, y, core)
    x_up = dev(lax.rem(x + 1, 4), zlo, zhi, y, core)
    x_dn = dev(lax.rem(x + 3, 4), zlo, zhi, y, core)
    z_up = dev(x, jnp.minimum(zlo + 1, 3), zhi, y, core)
    z_dn = dev(x, jnp.maximum(zlo - 1, 0), zhi, y, core)
    panel_dev = (zhi == 0) & (y < 2)

    def remote(src, dst, ss, rs, to):
        return pltpu.make_async_remote_copy(
            src_ref=src, dst_ref=dst, send_sem=ss, recv_sem=rs, device_id=to, device_id_type=MESH
        )

    def landed(ref, sem):
        pltpu.make_async_copy(ref, ref, sem).wait()

    bar = pltpu.get_barrier_semaphore()

    def greet(to):
        pl.semaphore_signal(bar, inc=1, device_id=to, device_id_type=MESH)

    for to in (y_up, y_dn, sib, part, x_up, x_dn):
        greet(to)

    @pl.when(zlo < 3)
    def _():
        greet(z_up)

    @pl.when(zlo > 0)
    def _():
        greet(z_dn)

    @pl.when(panel_dev)
    def _():
        def one(p, carry):
            peer = lax.rem(c, 2) * 8 + p

            @pl.when(peer != c)
            def _():
                greet((r, peer))

            return carry

        lax.fori_loop(0, 8, one, 0)

    expect = 6 + (zlo < 3).astype(jnp.int32) + (zlo > 0).astype(jnp.int32)
    from_panel = (n0 != c).astype(jnp.int32) + (n0 + 2 != c).astype(jnp.int32)
    expect = expect + jnp.where(zhi == 0, from_panel, 0)
    pl.semaphore_wait(bar, expect)

    child_copy = remote(contrib, cpart, x_s.at[0], x_recv.at[0], part)
    inv_copy = remote(inv, invx, x_s.at[1], x_recv.at[1], part)
    wrow = pl.ds(pl.multiple_of(lax.rem(c, 8) * 32, 32), 32)
    wslot = lax.rem(c, 8)

    def inverse_rows(src, which, owner, wait):
        for k in range(4):
            cols = pl.ds(k * BLK, BLK)

            @pl.when(k <= owner)
            def _(k=k, cols=cols):
                @pl.when(owner == c)
                def _():
                    if not wait:
                        wbuf[wrow, cols] = src[:, cols]

                @pl.when(owner != c)
                def _():
                    cp = remote(
                        src.at[:, cols], wbuf.at[wrow, cols],
                        w_s.at[which * 4 + k], w_recv.at[wslot * 4 + k], (r, owner),
                    )
                    if wait:
                        cp.wait_send()
                    else:
                        cp.start()

    @pl.when(zhi == 1)
    def _():
        @pl.when(y < 2)
        def _():
            child_copy.start()
            inv_copy.start()

        @pl.when(y >= 2)
        def _():
            inv_copy.start()
            child_copy.start()

    @pl.when(zhi == 0)
    def _():
        inverse_rows(inv, 0, n0, False)
        landed(invx, x_recv.at[1])
        inverse_rows(invx, 1, n0 + 2, False)

        @pl.when(y >= 2)
        def _():
            child_copy.start()

    scol = lax.rem(c, 16)

    def weight(h, i, j):
        hit = (cmap[h, r] == i * 16 + r) & (cmap[h, scol] == j * 32 + c)
        return jnp.where(hit, pattern[h * 16 + r, scol], 0).astype(F32)

    def base(i, j):
        return (
            front[i * 2 + j]
            + weight(zhi, i, j) * contrib[...]
            + weight(1 - zhi, i, j) * cpart[...]
        )

    def grp_rows(g):
        return pl.ds(pl.multiple_of(g * GRP, GRP), GRP)

    def pan_copy(k, g, kind, to):
        part_ref = pan.at[k, grp_rows(g)]
        return remote(part_ref, part_ref, a_s.at[kind], a_recv.at[k * 8 + g], to)

    @pl.when(panel_dev)
    def _():
        landed(cpart, x_recv.at[0])
        child_copy.start()
        for i in range(4):
            pan[c, pl.ds(i * BLK, BLK)] = base(i, 0)

        def send_all(to, kind):
            def one(g, carry):
                pan_copy(c, g, kind, to).start()
                return carry

            lax.fori_loop(0, 8, one, 0)

        @pl.when(y == 0)
        def _():
            send_all(y_up, 0)

        @pl.when(core == 0)
        def _():
            send_all(sib, 1)

        def piece(p, carry):
            for k in range(4):
                @pl.when((k <= c) & (lax.rem(c, 2) * 8 + p != c))
                def _(k=k):
                    landed(
                        wbuf.at[pl.ds(pl.multiple_of(p * 32, 32), 32), pl.ds(k * BLK, BLK)],
                        w_recv.at[p * 4 + k],
                    )

            return carry

        lax.fori_loop(0, 8, piece, 0)
        for k in range(4):
            @pl.when(k <= c)
            def _(k=k):
                hi, lo = split(wbuf[:, pl.ds(k * BLK, BLK)])
                wh[k] = hi
                wl[k] = lo

    def make_factor(g):
        @pl.when(y == 1)
        def _():
            @pl.when(core == 0)
            def _():
                landed(pan.at[0, grp_rows(g)], a_recv.at[g])
                pan_copy(0, g, 2, sib).start()
                landed(pan.at[1, grp_rows(g)], a_recv.at[8 + g])

            @pl.when(core == 1)
            def _():
                landed(pan.at[1, grp_rows(g)], a_recv.at[8 + g])
                pan_copy(1, g, 2, sib).start()
                landed(pan.at[0, grp_rows(g)], a_recv.at[g])
                landed(pan.at[2, grp_rows(g)], a_recv.at[16 + g])

        @pl.when((y == 0) & (core == 1))
        def _():
            landed(pan.at[0, grp_rows(g)], a_recv.at[g])

        def add(k, acc):
            ah, al = split(pan[k, grp_rows(g)])
            return acc + nt_dot(ah, wh[k]) + (nt_dot(ah, wl[k]) + nt_dot(al, wh[k]))

        fac[c, grp_rows(g)] = lax.fori_loop(0, c + 1, add, jnp.zeros((GRP, BLK), F32))

    xs = 2 * lax.rem(y, 2) + core
    zs = y // 2
    dxs = lax.rem(x - xs + 4, 4)
    dz = jnp.abs(zlo - zs)
    c_dist = dz + jnp.where(dxs == 3, 1, dxs)
    c_go = (
        ((zlo >= zs) & (zlo < 3) & (dxs == 0), z_up),
        ((zlo <= zs) & (zlo > 0) & (dxs == 0), z_dn),
        ((dxs == 0) | ((core == 1) & (dxs == 1)), x_up),
        ((dxs == 0) | ((core == 0) & (dxs == 3)), x_dn),
    )

    def position(s):
        return jnp.where(s == 0, lax.rem(8 - y, 8), lax.rem(y + 7, 8))

    def lag(hops, s):
        return (hops * HOP_NUM) // HOP_DEN + s * R_OFF

    def ch_rows(m):
        return pl.ds(pl.multiple_of(m * CH, CH), CH)

    def step(t, carry):
        @pl.when(panel_dev & (lax.rem(t - y * R_OFF + 16, 2) == 0) & (t >= y * R_OFF) & (t < NCH + y * R_OFF))
        def _():
            make_factor((t - y * R_OFF) // 2)

        def stream(sq, carry):
            s, q = sq // 4, lax.rem(sq, 4)
            pos = position(s)
            d = lax.rem(pos - q + 8, 8)
            hops = jnp.where(zhi == 0, pos, q + 1 + jnp.where(d <= 4, d, 8 - d))
            go_fwd = jnp.where(zhi == 0, pos < 7, d <= 3)
            go_rev = (zhi == 1) & ((d == 0) | (d >= 6))
            go_cross = (zhi == 0) & (pos == q)
            first = (zhi == 0) & (pos == 0)
            own, other = 2 * s + core, 2 * s + 1 - core

            def chunk_now(extra):
                m = t - lag(hops + extra, s)
                return m, (m >= 0) & (m < NCH) & (lax.rem(m + 64, 4) == q)

            m, now = chunk_now(0)

            @pl.when(now)
            def _():
                ref = fac.at[own, ch_rows(m)]
                sem = r_recv.at[own * NCH + m]

                @pl.when(jnp.logical_not(first))
                def _():
                    landed(ref, sem)

                @pl.when(go_fwd & (s == 0))
                def _():
                    remote(ref, ref, fwd_s.at[sq], sem, y_dn).start()

                @pl.when(go_fwd & (s == 1))
                def _():
                    remote(ref, ref, fwd_s.at[sq], sem, y_up).start()

                @pl.when(go_rev & (s == 0))
                def _():
                    remote(ref, ref, rev_s.at[sq], sem, y_up).start()

                @pl.when(go_rev & (s == 1))
                def _():
                    remote(ref, ref, rev_s.at[sq], sem, y_dn).start()

                @pl.when(go_cross)
                def _():
                    remote(ref, ref, cross_s.at[sq], sem, part).start()

                remote(ref, ref, sib_s.at[sq], sem, sib).start()

            m1, now1 = chunk_now(1)

            @pl.when(now1)
            def _():
                landed(fac.at[other, ch_rows(m1)], r_recv.at[other * NCH + m1])

            for n, extra in ((own, 0), (other, 1)):
                mc, nowc = chunk_now(extra + c_dist)
                slot = mc // PER_SLOT

                @pl.when(nowc & (lax.rem(slot, 2) == zhi))
                def _(n=n, mc=mc, slot=slot):
                    idx = (slot // 2) * PER_SLOT + lax.rem(mc, PER_SLOT)
                    dst = facc.at[n, ch_rows(idx)]
                    sem = c_recv.at[n * (NCH // 2) + idx]

                    @pl.when(c_dist == 0)
                    def _():
                        src = fac.at[n, ch_rows(mc)]
                        for kind, (go, to) in enumerate(c_go):
                            @pl.when(go)
                            def _(kind=kind, to=to):
                                remote(src, dst, c_s.at[kind * 4 + n], sem, to).start()

                    @pl.when(c_dist > 0)
                    def _():
                        landed(dst, sem)
                        for kind, (go, to) in enumerate(c_go):
                            @pl.when(go)
                            def _(kind=kind, to=to):
                                remote(dst, dst, c_s.at[kind * 4 + n], sem, to).start()

            return carry

        return lax.fori_loop(0, 8, stream, carry)

    lax.fori_loop(0, STEPS, step, 0)

    @pl.when(jnp.logical_not(panel_dev))
    def _():
        landed(cpart, x_recv.at[0])

    for n in range(4):
        cols = pl.ds(n * BLK, BLK)
        for i in range(4):
            rows = pl.ds(i * BLK, BLK)
            hi, lo = split(fac[n, rows])
            fh[rows, cols] = hi
            fl[rows, cols] = lo
        for j in range(2):
            rows = pl.ds(j * BLK, BLK)

            @pl.when(c_dist == 0)
            def _(n=n, j=j, rows=rows, cols=cols):
                at = pl.multiple_of((2 * j + zhi) * BLK, BLK)
                hi, lo = split(fac[n, pl.ds(at, BLK)])
                ch[rows, cols] = hi
                cl[rows, cols] = lo

            @pl.when(c_dist > 0)
            def _(n=n, j=j, rows=rows, cols=cols):
                hi, lo = split(facc[n, rows])
                ch[rows, cols] = hi
                cl[rows, cols] = lo

    def update(i, carry):
        rows = pl.ds(pl.multiple_of(i * BLK, BLK), BLK)
        for j in range(2):
            def trail(j=j):
                cr = pl.ds(j * BLK, BLK)
                u = nt_dot(fh[rows], ch[cr]) + (nt_dot(fh[rows], cl[cr]) + nt_dot(fl[rows], ch[cr]))
                on = ((i * 16 + r >= 4) & (j * 32 + c >= 4)).astype(jnp.int32).astype(F32)
                out[i * 2 + j] = base(i, j) - on * u

            if j == 0:
                pl.when(c >= 4)(trail)

                @pl.when(c < 4)
                def _():
                    out[i * 2] = fac[jnp.minimum(c, 3), rows]
            else:
                trail()
        return carry

    lax.fori_loop(0, 4, update, 0)

    def left(ref, sem):
        remote(ref, ref, sem, sem, sib).wait_send()

    def sent(sq, carry):
        s, q = sq // 4, lax.rem(sq, 4)
        pos = position(s)
        d = lax.rem(pos - q + 8, 8)
        quarter = fac.at[0, pl.ds(0, ROWS // 4)]

        @pl.when(jnp.where(zhi == 0, pos < 7, d <= 3))
        def _():
            left(quarter, fwd_s.at[sq])

        @pl.when((zhi == 1) & ((d == 0) | (d >= 6)))
        def _():
            left(quarter, rev_s.at[sq])

        @pl.when((zhi == 0) & (pos == q))
        def _():
            left(quarter, cross_s.at[sq])

        left(quarter, sib_s.at[sq])
        return carry

    lax.fori_loop(0, 8, sent, 0)
    for kind, (go, _to) in enumerate(c_go):
        for n in range(4):
            @pl.when(go)
            def _(kind=kind, n=n):
                left(facc.at[n], c_s.at[kind * 4 + n])

    child_copy.wait_send()

    @pl.when(zhi == 1)
    def _():
        inv_copy.wait_send()

    @pl.when(zhi == 0)
    def _():
        inverse_rows(inv, 0, n0, True)
        inverse_rows(invx, 1, n0 + 2, True)

    @pl.when(panel_dev)
    def _():
        @pl.when(y == 0)
        def _():
            left(pan.at[0], a_s.at[0])

        @pl.when(core == 0)
        def _():
            left(pan.at[0], a_s.at[1])

        @pl.when(y == 1)
        def _():
            left(pan.at[0], a_s.at[2])


def body(front, contrib, child_map, pattern, inverse):
    vm = pl.BlockSpec(memory_space=pltpu.VMEM)
    sm = pl.BlockSpec(memory_space=pltpu.SMEM)
    dma = pltpu.SemaphoreType.DMA
    front_t = front.transpose(0, 2, 1, 3).reshape(8, BLK, BLK)
    out = pl.pallas_call(
        kernel,
        out_shape=jax.ShapeDtypeStruct((8, BLK, BLK), F32),
        in_specs=[vm, vm, sm, sm, vm],
        out_specs=vm,
        scratch_shapes=[
            pltpu.VMEM((4, ROWS, BLK), F32),
            pltpu.VMEM((4, ROWS // 2, BLK), F32),
            pltpu.VMEM((4, ROWS, BLK), F32),
            pltpu.VMEM((BLK, BLK), F32),
            pltpu.VMEM((32, 1024), F32),
            pltpu.VMEM((BLK, 1024), F32),
            pltpu.VMEM((4, BLK, BLK), BF16),
            pltpu.VMEM((4, BLK, BLK), BF16),
            pltpu.VMEM((ROWS, 1024), BF16),
            pltpu.VMEM((ROWS, 1024), BF16),
            pltpu.VMEM((ROWS // 2, 1024), BF16),
            pltpu.VMEM((ROWS // 2, 1024), BF16),
            dma((4 * NCH,)),
            dma((4 * NCH // 2,)),
            dma((32,)),
            dma((32,)),
            dma((2,)),
            dma((8,)),
            dma((8,)),
            dma((8,)),
            dma((8,)),
            dma((16,)),
            dma((3,)),
            dma((8,)),
            dma((2,)),
        ],
        compiler_params=pltpu.CompilerParams(
            collective_id=0, has_side_effects=True, vmem_limit_bytes=48 << 20
        ),
        name="panel_step",
    )(front_t, contrib.reshape(BLK, BLK), child_map, pattern.reshape(32, 16), inverse)
    return out.reshape(4, 2, BLK, BLK).transpose(0, 2, 1, 3)


def solution(mesh):
    return jax.shard_map(
        body,
        mesh=mesh,
        in_specs=(
            P(None, "row", None, "col"),
            P(None, "row", None, "col"),
            P(),
            P(),
            P("col", None),
        ),
        out_specs=P(None, "row", None, "col"),
        check_vma=False,
    )
```

time: 726 us -> 132 us (0.18)
  the two profiles are of different devices: /device:TPU:8 before, /device:TPU:452 now
where the time goes in v1:
time: 132 us
  Pallas kernels  126 us (95%)
  local copies, waits for them, and re-layouts  5.77 us (4%)
    pallas_call x1, Pallas kernels, body(): pl.pallas_call(kernel, out_shape=jax.ShapeDtypeStruct((8, BLK, BLK), F32)...  126 us
    reshape x1, local copies, waits for them, and re-layouts, body(): return out.reshape(4, 2, BLK, BLK).transpose(0, 2, 1, 3)  2.94 us

profile of v1, /device:TPU:452, one launch (start us, length us, event | category | flops | bytes accessed | tf_op | source)
XLA Modules:
  0.0 131.6 jit_solution(6085214085978172824)
XLA Ops:
  0.0 1.0 copy.12
  1.0 0.0 copy-start
  1.0 0.0 copy-start.1
  1.0 0.0 copy-start.2
  1.0 1.8 %copy.6 = f32[4,2,256,256]{3,2,1,0:T(8,128)S(1)} copy(f32[4,2,256,256]{3,1,2,0:T(2,128)} %bitcast.14) | data formatting | bytes 4194304 | tf_op jit(solution)/shard_map/transpose | solution.py:459
  2.9 0.0 copy-done
  2.9 0.0 copy-done.1
  2.9 0.0 copy-done.2
  2.9 125.8 %panel_step.1 = f32[8,256,256]{2,1,0:T(8,128)S(1)} custom-call(f32[8,256,256]{2,1,0:T(8,128)S(1)} %bitcast.11, f32[256,256]{1,0:T(8,128)S(1)} %bitcast.12, s32[2,16]{1,0:T(2,128)S(1)} %copy-done.2, s32[32,16]{1,0:T(8,128)S(1)} %bitcast.13, f32[32,1024]{1,0:T(8,128)S(1)} %copy-done), custom_call_target="tpu_custom_call" | custom-call | tf_op jit(solution)/shard_map/panel_step/pallas_call | solution.py:460
  128.6 2.9 %copy.11 = f32[4,2,256,256]{3,1,2,0:T(2,128)} copy(f32[4,2,256,256]{3,2,1,0:T(8,128)S(1)} %bitcast.10) | data formatting | bytes 4194304 | tf_op jit(solution)/shard_map/reshape | solution.py:497
Async XLA Ops:
  1.0 1.9 %copy-start = (f32[32,1024]{1,0:T(8,128)S(1)}, f32[32,1024]{1,0:T(8,128)}, u32[]{:S(2)}) copy-start(f32[32,1024]{1,0:T(8,128)} %inv.1) | copy-start | bytes 393220
  1.0 1.9 %copy-start.1 = (s32[2,16,16]{2,1,0:T(8,128)S(1)}, s32[2,16,16]{2,1,0:T(8,128)}, u32[]{:S(2)}) copy-start(s32[2,16,16]{2,1,0:T(8,128)} %param.8) | copy-start | bytes 6148
  1.0 1.9 %copy-start.2 = (s32[2,16]{1,0:T(2,128)S(1)}, s32[2,16]{1,0:T(2,128)}, u32[]{:S(2)}) copy-start(s32[2,16]{1,0:T(2,128)} %cmap.1) | copy-start | bytes 388

commit v2 on v1

v2 whole, which is shorter than its diff:
```python
import functools

import jax
import jax.numpy as jnp
from jax import lax
from jax.experimental import pallas as pl
from jax.experimental.pallas import tpu as pltpu
from jax.sharding import PartitionSpec as P

MESH = pl.DeviceIdType.MESH
F32 = jnp.float32
BF16 = jnp.bfloat16

BLK = 256
ROWS = 1024
CH = 64
NCH = ROWS // CH
PER_SLOT = BLK // CH
HOP_NUM, HOP_DEN = 3, 1
R_OFF = 1
GRP = 128
PER_GRP = GRP // CH
C_SLACK = 0
AHEAD = 2


def nt_dot(a, b):
    return lax.dot_general(a, b, (((1,), (1,)), ((), ())), preferred_element_type=F32)


def split(x):
    hi = x.astype(BF16)
    return hi, (x - hi.astype(F32)).astype(BF16)


def kernel(
    front, contrib, cmap, pattern, inv, out,
    fac, facc, pan, cpart, invx, wbuf, wh, wl, fh, fl, ch, cl,
    r_recv, c_recv, a_recv, w_recv, x_recv,
    fwd_s, rev_s, cross_s, sib_s, c_s, a_s, w_s, x_s,
):
    r = lax.axis_index("row")
    c = lax.axis_index("col")
    x, zlo = lax.rem(r, 4), r // 4
    zhi, y, core = c // 16, lax.rem(c // 2, 8), lax.rem(c, 2)
    n0 = lax.rem(c, 16) // 8

    def dev(x_, zlo_, zhi_, y_, core_):
        return (zlo_ * 4 + x_, zhi_ * 16 + y_ * 2 + core_)

    y_up = dev(x, zlo, zhi, lax.rem(y + 1, 8), core)
    y_dn = dev(x, zlo, zhi, lax.rem(y + 7, 8), core)
    sib = dev(x, zlo, zhi, y, 1 - core)
    part = dev(x, zlo, 1 - zhi, y, core)
    mirror = dev(x, 3 - zlo, 1 - zhi, y, core)
    x_up = dev(lax.rem(x + 1, 4), zlo, zhi, y, core)
    x_dn = dev(lax.rem(x + 3, 4), zlo, zhi, y, core)
    z_up = dev(x, jnp.minimum(zlo + 1, 3), zhi, y, core)
    z_dn = dev(x, jnp.maximum(zlo - 1, 0), zhi, y, core)
    panel_dev = (zhi == 0) & (y < 2)

    def remote(src, dst, ss, rs, to):
        return pltpu.make_async_remote_copy(
            src_ref=src, dst_ref=dst, send_sem=ss, recv_sem=rs, device_id=to, device_id_type=MESH
        )

    def landed(ref, sem):
        pltpu.make_async_copy(ref, ref, sem).wait()

    bar = pltpu.get_barrier_semaphore()

    def greet(to):
        pl.semaphore_signal(bar, inc=1, device_id=to, device_id_type=MESH)

    for to in (y_up, y_dn, sib, part, mirror, x_up, x_dn):
        greet(to)

    @pl.when(zlo < 3)
    def _():
        greet(z_up)

    @pl.when(zlo > 0)
    def _():
        greet(z_dn)

    @pl.when(panel_dev)
    def _():
        def one(p, carry):
            peer = lax.rem(c, 2) * 8 + p

            @pl.when(peer != c)
            def _():
                greet((r, peer))

            return carry

        lax.fori_loop(0, 8, one, 0)

    expect = 7 + (zlo < 3).astype(jnp.int32) + (zlo > 0).astype(jnp.int32)
    from_panel = (n0 != c).astype(jnp.int32) + (n0 + 2 != c).astype(jnp.int32)
    expect = expect + jnp.where(zhi == 0, from_panel, 0)
    pl.semaphore_wait(bar, expect)

    child_copy = remote(contrib, cpart, x_s.at[0], x_recv.at[0], part)
    inv_copy = remote(inv, invx, x_s.at[1], x_recv.at[1], mirror)
    wrow = pl.ds(pl.multiple_of(lax.rem(c, 8) * 32, 32), 32)
    wslot = lax.rem(c, 8)

    def inverse_rows(src, which, owner, wait):
        for k in range(4):
            cols = pl.ds(k * BLK, BLK)

            @pl.when(k <= owner)
            def _(k=k, cols=cols):
                @pl.when(owner == c)
                def _():
                    if not wait:
                        wbuf[wrow, cols] = src[:, cols]

                @pl.when(owner != c)
                def _():
                    cp = remote(
                        src.at[:, cols], wbuf.at[wrow, cols],
                        w_s.at[which * 4 + k], w_recv.at[wslot * 4 + k], (r, owner),
                    )
                    if wait:
                        cp.wait_send()
                    else:
                        cp.start()

    @pl.when(zhi == 1)
    def _():
        @pl.when(y < 2)
        def _():
            child_copy.start()
            inv_copy.start()
            inv_copy.wait_send()

        @pl.when(y >= 2)
        def _():
            inv_copy.start()
            inv_copy.wait_send()
            child_copy.start()

    @pl.when(zhi == 0)
    def _():
        inverse_rows(inv, 0, n0, False)

        @pl.when(y >= 2)
        def _():
            landed(invx, x_recv.at[1])
            inverse_rows(invx, 1, n0 + 2, False)
            child_copy.start()

    scol = lax.rem(c, 16)

    def weight(h, i, j):
        hit = (cmap[h, r] == i * 16 + r) & (cmap[h, scol] == j * 32 + c)
        return jnp.where(hit, pattern[h * 16 + r, scol], 0).astype(F32)

    def base(i, j):
        return (
            front[i * 2 + j]
            + weight(zhi, i, j) * contrib[...]
            + weight(1 - zhi, i, j) * cpart[...]
        )

    def grp_rows(g):
        return pl.ds(pl.multiple_of(g * GRP, GRP), GRP)

    def pan_ref(k, g):
        return pan.at[grp_rows(g), pl.ds(pl.multiple_of(k * BLK, BLK), BLK)]

    def pan_copy(k, g, kind, to):
        part_ref = pan_ref(k, g)
        return remote(part_ref, part_ref, a_s.at[kind * 8 + g], a_recv.at[k * 8 + g], to)

    @pl.when(panel_dev)
    def _():
        landed(cpart, x_recv.at[0])
        for i in range(4):
            pan[pl.ds(i * BLK, BLK), pl.ds(pl.multiple_of(c * BLK, BLK), BLK)] = base(i, 0)

        landed(invx, x_recv.at[1])
        inverse_rows(invx, 1, n0 + 2, False)
        child_copy.start()

        def piece(p, carry):
            for k in range(4):
                @pl.when((k <= c) & (lax.rem(c, 2) * 8 + p != c))
                def _(k=k):
                    landed(
                        wbuf.at[pl.ds(pl.multiple_of(p * 32, 32), 32), pl.ds(k * BLK, BLK)],
                        w_recv.at[p * 4 + k],
                    )

            return carry

        lax.fori_loop(0, 8, piece, 0)
        for k in range(4):
            @pl.when(k <= c)
            def _(k=k):
                cols = pl.ds(k * BLK, BLK)
                hi, lo = split(wbuf[:, cols])
                wh[:, cols] = hi
                wl[:, cols] = lo

    def pass_panel(g):
        @pl.when(y == 0)
        def _():
            @pl.when(g >= AHEAD)
            def _():
                pan_copy(c, g - AHEAD, 0, y_up).wait_send()

            pan_copy(c, g, 0, y_up).start()

        @pl.when(core == 0)
        def _():
            pan_copy(c, g, 1, sib).start()

        for k in range(2):
            @pl.when((y == 1) & (core == k))
            def _(k=k):
                landed(pan_ref(k, g), a_recv.at[k * 8 + g])
                pan_copy(k, g, 2, sib).start()

    def make_factor(g):
        for n, waits in enumerate(((), (0,), (1,), (0, 2))):
            @pl.when(c == n)
            def _(n=n, waits=waits):
                for k in waits:
                    landed(pan_ref(k, g), a_recv.at[k * 8 + g])
                cols = pl.ds(0, (n + 1) * BLK)
                ah, al = split(pan[grp_rows(g), cols])
                w = wh[:, cols]
                fac[n, grp_rows(g)] = nt_dot(ah, w) + (nt_dot(ah, wl[:, cols]) + nt_dot(al, w))

    xs = 2 * lax.rem(y, 2) + core
    zs = y // 2
    dxs = lax.rem(x - xs + 4, 4)
    dz = jnp.abs(zlo - zs)
    c_dist = dz + jnp.where(dxs == 3, 1, dxs)
    c_go = (
        ((zlo >= zs) & (zlo < 3) & (dxs == 0), z_up),
        ((zlo <= zs) & (zlo > 0) & (dxs == 0), z_dn),
        ((dxs == 0) | ((core == 1) & (dxs == 1)), x_up),
        ((dxs == 0) | ((core == 0) & (dxs == 3)), x_dn),
    )

    def position(s):
        return lax.rem(8 - y, 8) if s == 0 else lax.rem(y + 7, 8)

    def lag(hops, s):
        return (hops * HOP_NUM) // HOP_DEN + s * R_OFF

    def ch_rows(m):
        return pl.ds(pl.multiple_of(m * CH, CH), CH)

    def fwd_to(s):
        return y_dn if s == 0 else y_up

    def rev_to(s):
        return y_up if s == 0 else y_dn

    def split_into(ref, hi_ref, lo_ref, rows, n):
        hi, lo = split(ref[...])
        cols = pl.ds(pl.multiple_of(n * BLK, BLK), BLK)
        hi_ref[rows, cols] = hi
        lo_ref[rows, cols] = lo

    def chunk_in(s, m, first, sends):
        own = 2 * s + core
        ref = fac.at[own, ch_rows(m)]
        sem = r_recv.at[own * NCH + m]
        if first is None:
            landed(ref, sem)
        else:
            pl.when(jnp.logical_not(first))(lambda: landed(ref, sem))
        for go, to, ss, before in sends:
            def start(to=to, ss=ss, before=before):
                if before is not None:
                    pl.when(m >= AHEAD)(remote(ref, ref, before, sem, to).wait_send)
                remote(ref, ref, ss, sem, to).start()

            pl.when(go)(start) if go is not None else start()
        split_into(ref, fh, fl, ch_rows(m), own)

    def sibling_in(s, m):
        n = 2 * s + 1 - core
        ref = fac.at[n, ch_rows(m)]
        landed(ref, r_recv.at[n * NCH + m])
        split_into(ref, fh, fl, ch_rows(m), n)

    def column_in(n, m):
        idx = m // (2 * PER_SLOT) * PER_SLOT + lax.rem(m, PER_SLOT)
        dst = facc.at[n, ch_rows(idx)]
        sem = c_recv.at[n * (NCH // 2) + idx]

        def go_on(src):
            for kind, (go, to) in enumerate(c_go):
                @pl.when(go)
                def _(kind=kind, to=to):
                    remote(src, dst, c_s.at[kind * 4 + n], sem, to).start()

            split_into(src, ch, cl, ch_rows(idx), n)

        @pl.when(c_dist == 0)
        def _():
            go_on(fac.at[n, ch_rows(m)])

        @pl.when(c_dist > 0)
        def _():
            landed(dst, sem)
            go_on(dst)

    def update(i, j):
        rows = pl.ds(pl.multiple_of(i * BLK, BLK), BLK)
        cr = pl.ds(j * BLK, BLK)
        u = nt_dot(fh[rows], ch[cr]) + (nt_dot(fh[rows], cl[cr]) + nt_dot(fl[rows], ch[cr]))
        on = ((i * 16 + r >= 4) & (j * 32 + c >= 4)).astype(jnp.int32).astype(F32)
        out[i * 2 + j] = base(i, j) - on * u

    def first_update(k):
        @pl.when((k == 0) & jnp.logical_not(panel_dev))
        def _():
            landed(cpart, x_recv.at[0])

        @pl.when(c >= 4)
        def _():
            update(k, 0)

        @pl.when(c < 4)
        def _():
            out[k * 2] = fac[jnp.minimum(c, 3), pl.ds(pl.multiple_of(k * BLK, BLK), BLK)]

    def within(m):
        return (m >= 0) & (m < NCH)

    def most(values):
        return functools.reduce(jnp.maximum, values)

    slack = jnp.where(c_dist > 0, C_SLACK, 0)

    def loop(half, lags, body):
        r_end = NCH + most([lags[k](1) for k in lags])
        c_end = most([lags[k](1 + c_dist) for k in lags]) + slack
        c0_end = PER_SLOT * (1 + half) + c_end
        end = NCH + c_end
        upd = jnp.maximum(r_end, c0_end)

        def step(t, carry):
            body(t)

            @pl.when((t >= upd) & (t < upd + 4))
            def _():
                first_update(t - upd)

            return carry

        lax.fori_loop(0, jnp.maximum(end, upd + 4), step, 0)

    @pl.when(zhi == 0)
    def _():
        pos = [position(0), position(1)]
        lags = {s: (lambda extra, s=s: lag(pos[s] + extra, s)) for s in (0, 1)}
        at = [[lags[s](e) for e in (0, 1)] + [lags[s](e + c_dist) + slack for e in (0, 1)] for s in (0, 1)]
        lead = y * R_OFF

        def body(t):
            g = t - lead

            @pl.when(panel_dev & within(t) & (lax.rem(t, PER_GRP) == 0))
            def _():
                pass_panel(t // PER_GRP)

            @pl.when(panel_dev & within(g) & (lax.rem(g, PER_GRP) == 0))
            def _():
                make_factor(g // PER_GRP)

            for s in (0, 1):
                m = t - at[s][0]

                @pl.when(within(m))
                def _(s=s, m=m):
                    q = 3 - lax.rem(m, 4)
                    chunk_in(s, m, pos[s] == 0, (
                        (pos[s] < 7, fwd_to(s), fwd_s.at[s * NCH + m],
                         fwd_s.at[s * NCH + jnp.maximum(m - AHEAD, 0)]),
                        (pos[s] == q, part, cross_s.at[s * 4 + q], None),
                        (None, sib, sib_s.at[s * 4 + q], None),
                    ))

                m1 = t - at[s][1]
                pl.when(within(m1))(functools.partial(sibling_in, s, m1))
                for e, n in ((0, 2 * s + core), (1, 2 * s + 1 - core)):
                    mc = t - at[s][2 + e]
                    pl.when(within(mc) & (lax.rem(mc // PER_SLOT, 2) == 0))(
                        functools.partial(column_in, n, mc)
                    )

        loop(0, lags, body)

    @pl.when(zhi == 1)
    def _():
        lags, at, info = {}, {}, {}
        for s in (0, 1):
            for q in range(4):
                d = lax.rem(position(s) - q + 8, 8)
                hops = q + 1 + jnp.where(d <= 4, d, 8 - d)
                lags[s, q] = lambda extra, s=s, hops=hops: lag(hops + extra, s)
                at[s, q] = [lags[s, q](e) for e in (0, 1)] + [
                    lags[s, q](e + c_dist) + slack for e in (0, 1)
                ]
                info[s, q] = (d <= 3, (d == 0) | (d >= 6))

        def body(t):
            for s in (0, 1):
                for q in range(4):
                    def mine(m, q=q):
                        return within(m) & (lax.rem(m + 16, 4) == 3 - q)

                    go_fwd, go_rev = info[s, q]
                    m = t - at[s, q][0]

                    @pl.when(mine(m))
                    def _(s=s, q=q, m=m, go_fwd=go_fwd, go_rev=go_rev):
                        chunk_in(s, m, None, (
                            (go_fwd, fwd_to(s), fwd_s.at[s * 4 + q], None),
                            (go_rev, rev_to(s), rev_s.at[s * 4 + q], None),
                            (None, sib, sib_s.at[s * 4 + q], None),
                        ))

                    m1 = t - at[s, q][1]
                    pl.when(mine(m1))(functools.partial(sibling_in, s, m1))
                    for e, n in ((0, 2 * s + core), (1, 2 * s + 1 - core)):
                        mc = t - at[s, q][2 + e]
                        pl.when(mine(mc) & (lax.rem(mc // PER_SLOT, 2) == 1))(
                            functools.partial(column_in, n, mc)
                        )

        loop(1, lags, body)

    def last_update(i, carry):
        update(i, 1)
        return carry

    lax.fori_loop(0, 4, last_update, 0)

    def left(ref, sem):
        remote(ref, ref, sem, sem, sib).wait_send()

    def sent(sq, carry):
        s, q = sq // 4, lax.rem(sq, 4)
        pos = jnp.where(s == 0, position(0), position(1))
        d = lax.rem(pos - q + 8, 8)
        quarter = fac.at[0, pl.ds(0, ROWS // 4)]

        @pl.when((zhi == 1) & (d <= 3))
        def _():
            left(quarter, fwd_s.at[sq])

        @pl.when((zhi == 0) & (pos < 7) & (q < AHEAD))
        def _():
            left(fac.at[0, ch_rows(0)], fwd_s.at[s * NCH + NCH - 1 - q])

        @pl.when((zhi == 1) & ((d == 0) | (d >= 6)))
        def _():
            left(quarter, rev_s.at[sq])

        @pl.when((zhi == 0) & (pos == q))
        def _():
            left(quarter, cross_s.at[sq])

        left(quarter, sib_s.at[sq])
        return carry

    lax.fori_loop(0, 8, sent, 0)
    for kind, (go, _to) in enumerate(c_go):
        for n in range(4):
            @pl.when(go)
            def _(kind=kind, n=n):
                left(facc.at[n], c_s.at[kind * 4 + n])

    child_copy.wait_send()

    @pl.when(zhi == 0)
    def _():
        inverse_rows(inv, 0, n0, True)
        inverse_rows(invx, 1, n0 + 2, True)

    @pl.when(panel_dev)
    def _():
        def one(g, carry):
            @pl.when((y == 0) & (g >= 8 - AHEAD))
            def _():
                pan_copy(c, g, 0, y_up).wait_send()

            @pl.when(core == 0)
            def _():
                pan_copy(c, g, 1, sib).wait_send()

            @pl.when(y == 1)
            def _():
                pan_copy(core, g, 2, sib).wait_send()

            return carry

        lax.fori_loop(0, 8, one, 0)


def body(front, contrib, child_map, pattern, inverse):
    vm = pl.BlockSpec(memory_space=pltpu.VMEM)
    sm = pl.BlockSpec(memory_space=pltpu.SMEM)
    dma = pltpu.SemaphoreType.DMA
    front_t = front.transpose(0, 2, 1, 3).reshape(8, BLK, BLK)
    out = pl.pallas_call(
        kernel,
        out_shape=jax.ShapeDtypeStruct((8, BLK, BLK), F32),
        in_specs=[vm, vm, sm, sm, vm],
        out_specs=vm,
        scratch_shapes=[
            pltpu.VMEM((4, ROWS, BLK), F32),
            pltpu.VMEM((4, ROWS // 2, BLK), F32),
            pltpu.VMEM((ROWS, 1024), F32),
            pltpu.VMEM((BLK, BLK), F32),
            pltpu.VMEM((32, 1024), F32),
            pltpu.VMEM((BLK, 1024), F32),
            pltpu.VMEM((BLK, 1024), BF16),
            pltpu.VMEM((BLK, 1024), BF16),
            pltpu.VMEM((ROWS, 1024), BF16),
            pltpu.VMEM((ROWS, 1024), BF16),
            pltpu.VMEM((ROWS // 2, 1024), BF16),
            pltpu.VMEM((ROWS // 2, 1024), BF16),
            dma((4 * NCH,)),
            dma((4 * NCH // 2,)),
            dma((32,)),
            dma((32,)),
            dma((2,)),
            dma((2 * NCH,)),
            dma((8,)),
            dma((8,)),
            dma((8,)),
            dma((16,)),
            dma((24,)),
            dma((8,)),
            dma((2,)),
        ],
        compiler_params=pltpu.CompilerParams(
            collective_id=0, has_side_effects=True, vmem_limit_bytes=48 << 20
        ),
        name="panel_step",
    )(front_t, contrib.reshape(BLK, BLK), child_map, pattern.reshape(32, 16), inverse)
    return out.reshape(4, 2, BLK, BLK).transpose(0, 2, 1, 3)


def solution(mesh):
    return jax.shard_map(
        body,
        mesh=mesh,
        in_specs=(
            P(None, "row", None, "col"),
            P(None, "row", None, "col"),
            P(),
            P(),
            P("col", None),
        ),
        out_specs=P(None, "row", None, "col"),
        check_vma=False,
    )
```

time: 132 us -> 119 us (0.902)
  the two profiles are of different devices: /device:TPU:452 before, /device:TPU:456 now
where the time goes in v2:
time: 119 us
  Pallas kernels  113 us (95%)
  local copies, waits for them, and re-layouts  5.77 us (5%)
    pallas_call x1, Pallas kernels, body(): pl.pallas_call(kernel, out_shape=jax.ShapeDtypeStruct((8, BLK, BLK), F32)...  113 us
    reshape x1, local copies, waits for them, and re-layouts, body(): return out.reshape(4, 2, BLK, BLK).transpose(0, 2, 1, 3)  2.94 us

profile of v2, /device:TPU:456, one launch (start us, length us, event | category | flops | bytes accessed | tf_op | source)
XLA Modules:
  0.0 118.6 jit_solution(13335560879447202330)
XLA Ops:
  0.0 1.0 copy.12
  1.0 0.0 copy-start
  1.0 0.0 copy-start.1
  1.0 0.0 copy-start.2
  1.0 1.8 %copy.6 = f32[4,2,256,256]{3,2,1,0:T(8,128)S(1)} copy(f32[4,2,256,256]{3,1,2,0:T(2,128)} %bitcast.14) | data formatting | bytes 4194304 | tf_op jit(solution)/shard_map/transpose | solution.py:515
  2.9 0.0 copy-done
  2.9 0.0 copy-done.1
  2.9 0.0 copy-done.2
  2.9 112.8 %panel_step.1 = f32[8,256,256]{2,1,0:T(8,128)S(1)} custom-call(f32[8,256,256]{2,1,0:T(8,128)S(1)} %bitcast.11, f32[256,256]{1,0:T(8,128)S(1)} %bitcast.12, s32[2,16]{1,0:T(2,128)S(1)} %copy-done.2, s32[32,16]{1,0:T(8,128)S(1)} %bitcast.13, f32[32,1024]{1,0:T(8,128)S(1)} %copy-done), custom_call_target="tpu_custom_call" | custom-call | tf_op jit(solution)/shard_map/panel_step/pallas_call | solution.py:516
  115.7 2.9 %copy.11 = f32[4,2,256,256]{3,1,2,0:T(2,128)} copy(f32[4,2,256,256]{3,2,1,0:T(8,128)S(1)} %bitcast.10) | data formatting | bytes 4194304 | tf_op jit(solution)/shard_map/reshape | solution.py:553
Async XLA Ops:
  1.0 1.9 %copy-start = (f32[32,1024]{1,0:T(8,128)S(1)}, f32[32,1024]{1,0:T(8,128)}, u32[]{:S(2)}) copy-start(f32[32,1024]{1,0:T(8,128)} %inv.1) | copy-start | bytes 393220
  1.0 1.9 %copy-start.1 = (s32[2,16,16]{2,1,0:T(8,128)S(1)}, s32[2,16,16]{2,1,0:T(8,128)}, u32[]{:S(2)}) copy-start(s32[2,16,16]{2,1,0:T(8,128)} %param.8) | copy-start | bytes 6148
  1.0 1.9 %copy-start.2 = (s32[2,16]{1,0:T(2,128)S(1)}, s32[2,16]{1,0:T(2,128)}, u32[]{:S(2)}) copy-start(s32[2,16]{1,0:T(2,128)} %cmap.1) | copy-start | bytes 388

commit v3 on v2

--- a/solution.py
+++ b/solution.py
@@ -20,6 +20,7 @@
 R_OFF = 1
 GRP = 128
 PER_GRP = GRP // CH
+TAIL = 1024
 C_SLACK = 0
 AHEAD = 2
 
@@ -37,7 +38,7 @@
     front, contrib, cmap, pattern, inv, out,
     fac, facc, pan, cpart, invx, wbuf, wh, wl, fh, fl, ch, cl,
     r_recv, c_recv, a_recv, w_recv, x_recv,
-    fwd_s, rev_s, cross_s, sib_s, c_s, a_s, w_s, x_s,
+    fwd_s, rev_s, cross_s, sib_s, c_s, h_s, a_s, w_s, x_s,
 ):
     r = lax.axis_index("row")
     c = lax.axis_index("col")
@@ -57,6 +58,7 @@
     x_dn = dev(lax.rem(x + 3, 4), zlo, zhi, y, core)
     z_up = dev(x, jnp.minimum(zlo + 1, 3), zhi, y, core)
     z_dn = dev(x, jnp.maximum(zlo - 1, 0), zhi, y, core)
+    across = tuple((to[0], to[1] + 1 - 2 * core) for to in (z_up, z_dn, x_up, x_dn))
     panel_dev = (zhi == 0) & (y < 2)
 
     def remote(src, dst, ss, rs, to):
@@ -72,16 +74,18 @@
     def greet(to):
         pl.semaphore_signal(bar, inc=1, device_id=to, device_id_type=MESH)
 
-    for to in (y_up, y_dn, sib, part, mirror, x_up, x_dn):
+    for to in (y_up, y_dn, sib, part, mirror, x_up, x_dn) + across[2:]:
         greet(to)
 
     @pl.when(zlo < 3)
     def _():
         greet(z_up)
+        greet(across[0])
 
     @pl.when(zlo > 0)
     def _():
         greet(z_dn)
+        greet(across[1])
 
     @pl.when(panel_dev)
     def _():
@@ -96,7 +100,7 @@
 
         lax.fori_loop(0, 8, one, 0)
 
-    expect = 7 + (zlo < 3).astype(jnp.int32) + (zlo > 0).astype(jnp.int32)
+    expect = 9 + 2 * (zlo < 3).astype(jnp.int32) + 2 * (zlo > 0).astype(jnp.int32)
     from_panel = (n0 != c).astype(jnp.int32) + (n0 + 2 != c).astype(jnp.int32)
     expect = expect + jnp.where(zhi == 0, from_panel, 0)
     pl.semaphore_wait(bar, expect)
@@ -246,6 +250,9 @@
         ((dxs == 0) | ((core == 1) & (dxs == 1)), x_up),
         ((dxs == 0) | ((core == 0) & (dxs == 3)), x_dn),
     )
+
+    helps = (zlo == zs) & (x == 2 * lax.rem(y, 2) + 1 - core)
+    help_go = (zlo < 3, zlo > 0, None, None)
 
     def position(s):
         return lax.rem(8 - y, 8) if s == 0 else lax.rem(y + 7, 8)
@@ -285,19 +292,33 @@
             pl.when(go)(start) if go is not None else start()
         split_into(ref, fh, fl, ch_rows(m), own)
 
+    def col_index(m):
+        return (m & (2 * PER_SLOT)) // 2 + (m & (PER_SLOT - 1))
+
+    def help_out(s, m):
+        n, idx = 2 * s + core, col_index(m)
+        for kind, (go, to) in enumerate(zip(help_go, across)):
+            def start(kind=kind, to=to):
+                remote(
+                    fac.at[n, ch_rows(m)], facc.at[n, ch_rows(idx)],
+                    h_s.at[kind * 2 + s], c_recv.at[n * (NCH // 2) + idx], to,
+                ).start()
+
+            start() if go is None else pl.when(go)(start)
+
     def sibling_in(s, m):
         n = 2 * s + 1 - core
         ref = fac.at[n, ch_rows(m)]
         landed(ref, r_recv.at[n * NCH + m])
         split_into(ref, fh, fl, ch_rows(m), n)
 
-    def column_in(n, m):
-        idx = m // (2 * PER_SLOT) * PER_SLOT + lax.rem(m, PER_SLOT)
+    def column_in(n, m, own):
+        idx = col_index(m)
         dst = facc.at[n, ch_rows(idx)]
         sem = c_recv.at[n * (NCH // 2) + idx]
 
-        def go_on(src):
-            for kind, (go, to) in enumerate(c_go):
+        def go_on(src, send):
+            for kind, (go, to) in enumerate(c_go if send else ()):
                 @pl.when(go)
                 def _(kind=kind, to=to):
                     remote(src, dst, c_s.at[kind * 4 + n], sem, to).start()
@@ -306,12 +327,12 @@
 
         @pl.when(c_dist == 0)
         def _():
-            go_on(fac.at[n, ch_rows(m)])
+            go_on(fac.at[n, ch_rows(m)], own)
 
         @pl.when(c_dist > 0)
         def _():
             landed(dst, sem)
-            go_on(dst)
+            go_on(dst, True)
 
     def update(i, j):
         rows = pl.ds(pl.multiple_of(i * BLK, BLK), BLK)
@@ -334,7 +355,7 @@
             out[k * 2] = fac[jnp.minimum(c, 3), pl.ds(pl.multiple_of(k * BLK, BLK), BLK)]
 
     def within(m):
-        return (m >= 0) & (m < NCH)
+        return (m & -NCH) == 0
 
     def most(values):
         return functools.reduce(jnp.maximum, values)
@@ -343,7 +364,7 @@
 
     def loop(half, lags, body):
         r_end = NCH + most([lags[k](1) for k in lags])
-        c_end = most([lags[k](1 + c_dist) for k in lags]) + slack
+        c_end = most([lags[k](jnp.maximum(c_dist, 1)) for k in lags]) + slack
         c0_end = PER_SLOT * (1 + half) + c_end
         end = NCH + c_end
         upd = jnp.maximum(r_end, c0_end)
@@ -351,7 +372,7 @@
         def step(t, carry):
             body(t)
 
-            @pl.when((t >= upd) & (t < upd + 4))
+            @pl.when(((t - upd) & -4) == 0)
             def _():
                 first_update(t - upd)
 
@@ -363,17 +384,17 @@
     def _():
         pos = [position(0), position(1)]
         lags = {s: (lambda extra, s=s: lag(pos[s] + extra, s)) for s in (0, 1)}
-        at = [[lags[s](e) for e in (0, 1)] + [lags[s](e + c_dist) + slack for e in (0, 1)] for s in (0, 1)]
+        at = [[lags[s](e) for e in (0, 1)] + [lags[s](jnp.maximum(c_dist, e)) + slack for e in (0, 1)] for s in (0, 1)]
         lead = y * R_OFF
 
         def body(t):
             g = t - lead
 
-            @pl.when(panel_dev & within(t) & (lax.rem(t, PER_GRP) == 0))
+            @pl.when(panel_dev & within(t) & ((t & (PER_GRP - 1)) == 0))
             def _():
                 pass_panel(t // PER_GRP)
 
-            @pl.when(panel_dev & within(g) & (lax.rem(g, PER_GRP) == 0))
+            @pl.when(panel_dev & within(g) & ((g & (PER_GRP - 1)) == 0))
             def _():
                 make_factor(g // PER_GRP)
 
@@ -382,20 +403,23 @@
 
                 @pl.when(within(m))
                 def _(s=s, m=m):
-                    q = 3 - lax.rem(m, 4)
+                    q = 3 - (m & 3)
                     chunk_in(s, m, pos[s] == 0, (
                         (pos[s] < 7, fwd_to(s), fwd_s.at[s * NCH + m],
                          fwd_s.at[s * NCH + jnp.maximum(m - AHEAD, 0)]),
                         (pos[s] == q, part, cross_s.at[s * 4 + q], None),
                         (None, sib, sib_s.at[s * 4 + q], None),
                     ))
+                    pl.when(helps & ((m & PER_SLOT) == 0))(
+                        functools.partial(help_out, s, m)
+                    )
 
                 m1 = t - at[s][1]
                 pl.when(within(m1))(functools.partial(sibling_in, s, m1))
                 for e, n in ((0, 2 * s + core), (1, 2 * s + 1 - core)):
                     mc = t - at[s][2 + e]
-                    pl.when(within(mc) & (lax.rem(mc // PER_SLOT, 2) == 0))(
-                        functools.partial(column_in, n, mc)
+                    pl.when((mc & -(2 * BLK // CH + PER_SLOT)) == 0)(
+                        functools.partial(column_in, n, mc, e == 0)
                     )
 
         loop(0, lags, body)
@@ -408,43 +432,46 @@
                 d = lax.rem(position(s) - q + 8, 8)
                 hops = q + 1 + jnp.where(d <= 4, d, 8 - d)
                 lags[s, q] = lambda extra, s=s, hops=hops: lag(hops + extra, s)
-                at[s, q] = [lags[s, q](e) for e in (0, 1)] + [
-                    lags[s, q](e + c_dist) + slack for e in (0, 1)
+                at[s, q] = [lags[s, q](e) + 3 - q for e in (0, 1)] + [
+                    lags[s, q](jnp.maximum(c_dist, e)) + slack + 3 - q for e in (0, 1)
                 ]
                 info[s, q] = (d <= 3, (d == 0) | (d >= 6))
 
         def body(t):
             for s in (0, 1):
                 for q in range(4):
-                    def mine(m, q=q):
-                        return within(m) & (lax.rem(m + 16, 4) == 3 - q)
-
                     go_fwd, go_rev = info[s, q]
+                    k = 3 - q
                     m = t - at[s, q][0]
 
-                    @pl.when(mine(m))
-                    def _(s=s, q=q, m=m, go_fwd=go_fwd, go_rev=go_rev):
+                    @pl.when((m & -13) == 0)
+                    def _(s=s, q=q, m=m + k, go_fwd=go_fwd, go_rev=go_rev):
                         chunk_in(s, m, None, (
                             (go_fwd, fwd_to(s), fwd_s.at[s * 4 + q], None),
                             (go_rev, rev_to(s), rev_s.at[s * 4 + q], None),
                             (None, sib, sib_s.at[s * 4 + q], None),
                         ))
+                        pl.when(helps & ((m & PER_SLOT) != 0))(functools.partial(help_out, s, m))
 
                     m1 = t - at[s, q][1]
-                    pl.when(mine(m1))(functools.partial(sibling_in, s, m1))
+                    pl.when((m1 & -13) == 0)(functools.partial(sibling_in, s, m1 + k))
                     for e, n in ((0, 2 * s + core), (1, 2 * s + 1 - core)):
                         mc = t - at[s, q][2 + e]
-                        pl.when(mine(mc) & (lax.rem(mc // PER_SLOT, 2) == 1))(
-                            functools.partial(column_in, n, mc)
-                        )
+                        pl.when((mc & -9) == 4)(functools.partial(column_in, n, mc + k, e == 0))
 
         loop(1, lags, body)
 
-    def last_update(i, carry):
-        update(i, 1)
+    def last_update(k, carry):
+        rows = pl.ds(pl.multiple_of(k * TAIL, TAIL), TAIL)
+        cr = pl.ds(BLK, BLK)
+        u = nt_dot(fh[rows], ch[cr]) + (nt_dot(fh[rows], cl[cr]) + nt_dot(fl[rows], ch[cr]))
+        for p in range(TAIL // BLK):
+            i = k * (TAIL // BLK) + p
+            on = (i * 16 + r >= 4).astype(jnp.int32).astype(F32)
+            out[i * 2 + 1] = base(i, 1) - on * u[p * BLK : (p + 1) * BLK]
         return carry
 
-    lax.fori_loop(0, 4, last_update, 0)
+    lax.fori_loop(0, ROWS // TAIL, last_update, 0)
 
     def left(ref, sem):
         remote(ref, ref, sem, sem, sib).wait_send()
@@ -477,9 +504,15 @@
     lax.fori_loop(0, 8, sent, 0)
     for kind, (go, _to) in enumerate(c_go):
         for n in range(4):
-            @pl.when(go)
+            @pl.when(go & ((c_dist > 0) | (core == n % 2)))
             def _(kind=kind, n=n):
                 left(facc.at[n], c_s.at[kind * 4 + n])
+
+    for kind, go in enumerate(help_go):
+        for n in range(2):
+            @pl.when(helps if go is None else helps & go)
+            def _(kind=kind, n=n):
+                left(facc.at[n], h_s.at[kind * 2 + n])
 
     child_copy.wait_send()
 
@@ -541,6 +574,7 @@
             dma((8,)),
             dma((8,)),
             dma((16,)),
+            dma((8,)),
             dma((24,)),
             dma((8,)),
             dma((2,)),

time: 119 us -> 119 us (level)
  the two profiles are of different devices: /device:TPU:456 before, /device:TPU:452 now
where the time goes in v3:
time: 119 us
  Pallas kernels  113 us (95%)
  local copies, waits for them, and re-layouts  5.77 us (5%)
    pallas_call x1, Pallas kernels, body(): pl.pallas_call(kernel, out_shape=jax.ShapeDtypeStruct((8, BLK, BLK), F32)...  113 us
    reshape x1, local copies, waits for them, and re-layouts, body(): return out.reshape(4, 2, BLK, BLK).transpose(0, 2, 1, 3)  2.94 us

profile of v3, /device:TPU:452, one launch (start us, length us, event | category | flops | bytes accessed | tf_op | source)
XLA Modules:
  0.0 118.9 jit_solution(15291869015000167509)
XLA Ops:
  0.0 1.0 copy.12
  1.0 0.0 copy-start
  1.0 0.0 copy-start.1
  1.0 0.0 copy-start.2
  1.0 1.8 %copy.6 = f32[4,2,256,256]{3,2,1,0:T(8,128)S(1)} copy(f32[4,2,256,256]{3,1,2,0:T(2,128)} %bitcast.14) | data formatting | bytes 4194304 | tf_op jit(solution)/shard_map/transpose | solution.py:548
  2.9 0.0 copy-done
  2.9 0.0 copy-done.1
  2.9 0.0 copy-done.2
  2.9 113.0 %panel_step.1 = f32[8,256,256]{2,1,0:T(8,128)S(1)} custom-call(f32[8,256,256]{2,1,0:T(8,128)S(1)} %bitcast.11, f32[256,256]{1,0:T(8,128)S(1)} %bitcast.12, s32[2,16]{1,0:T(2,128)S(1)} %copy-done.2, s32[32,16]{1,0:T(8,128)S(1)} %bitcast.13, f32[32,1024]{1,0:T(8,128)S(1)} %copy-done), custom_call_target="tpu_custom_call" | custom-call | tf_op jit(solution)/shard_map/panel_step/pallas_call | solution.py:549
  115.9 2.9 %copy.11 = f32[4,2,256,256]{3,1,2,0:T(2,128)} copy(f32[4,2,256,256]{3,2,1,0:T(8,128)S(1)} %bitcast.10) | data formatting | bytes 4194304 | tf_op jit(solution)/shard_map/reshape | solution.py:587
Async XLA Ops:
  1.0 1.9 %copy-start = (f32[32,1024]{1,0:T(8,128)S(1)}, f32[32,1024]{1,0:T(8,128)}, u32[]{:S(2)}) copy-start(f32[32,1024]{1,0:T(8,128)} %inv.1) | copy-start | bytes 393220
  1.0 1.9 %copy-start.1 = (s32[2,16,16]{2,1,0:T(8,128)S(1)}, s32[2,16,16]{2,1,0:T(8,128)}, u32[]{:S(2)}) copy-start(s32[2,16,16]{2,1,0:T(8,128)} %param.8) | copy-start | bytes 6148
  1.0 1.9 %copy-start.2 = (s32[2,16]{1,0:T(2,128)S(1)}, s32[2,16]{1,0:T(2,128)}, u32[]{:S(2)}) copy-start(s32[2,16]{1,0:T(2,128)} %cmap.1) | copy-start | bytes 388
